TPU v7x, 128 devices: a whole 4x4x4 slice. The times are simulated.
128 devices in a mesh: inst: 8 (over z, y_lo), slab: 16 (over y_hi, x, core).
Axes of the slice: x: 4, y: 4 (y_hi: 2, y_lo: 2; y = y_hi * 2 + y_lo), z: 4, core: 2. Of those that a mesh axis runs over, the one named last changes fastest.
Arguments:
- state: bfloat16 [16, 625, 8192], P('inst', None, 'slab'), may hold values from -6 to 6
- volume: float32 [8192], P('slab'), may hold values from 0.5 to 2
- step_size: float32 [8192], P('slab'), may hold values from 0.1 to 0.5
- stiffness: bfloat16 [625, 625], replicated, may hold values from -0.25 to 0.25
- face_coupling: bfloat16 [6, 625, 625], replicated, may hold values from -0.25 to 0.25
- precond: bfloat16 [625, 625], replicated, may hold values from -0.25 to 0.25
- mode_shapes: bfloat16 [8, 625, 8192], P(None, None, 'slab'), may hold values from -2 to 2
- amplitudes: float32 [16, 8], P('inst'), may hold values from -6 to 6
- surface_owner: int32 [8192], replicated, may hold values from 0 to 8191, as said below
- face_links: int32 [6, 8192], P(None, 'slab'), may hold values from 0 to 639
Outputs:
- residual: float32 [16, 625, 8192], P('inst', None, 'slab')
- new_state: float32 [16, 625, 8192], P('inst', None, 'slab')
Inputs may be any that keep to these rules, and one draw needn't show every extreme that they name: Surface rows r with r // 512 = s are held by slab s; of the rows of each slab, exactly 32 act on elements of each slab (surface_owner // 512).
All inputs are finite; a program needn't handle non-finite values.
Results may differ from a plain program's by a relative error of at most 0.0023.
Values may be sent and summed in bfloat16 or wider, within the bound.
A program may use at most 128 MiB of HBM per device.

v0:
```python
import functools

import jax
import jax.numpy as jnp
import numpy as np
from jax import lax
from jax.experimental import pallas as pl
from jax.experimental.pallas import tpu as pltpu
from jax.sharding import PartitionSpec as P

MESH = pl.DeviceIdType.MESH
F32, BF16 = jnp.float32, jnp.bfloat16

NB = 625
NBP = 640
GRP = 80
LAST = NB - 7 * GRP
NE = 512
HALVES = ((0, 48), (48, 32))
FIRST_FACES = 3


def derivative_blocks():
    n = np.arange(16)
    d = n[:, None] - n[None, :]
    safe = np.where(d == 0, 1, d)
    value = np.where(d == 0, 0.0, 0.2 * (-1.0) ** d / np.tan(np.pi * safe / 16))
    value = np.kron(value, np.eye(16)).astype(np.float32)
    high = value.astype(jnp.bfloat16)
    low = (value - high.astype(np.float32)).astype(jnp.bfloat16)
    return np.stack([high, low])


def dot(a, b):
    return jnp.dot(a, b, preferred_element_type=F32)


def dot_nt(a, b):
    return lax.dot_general(a, b, (((1,), (1,)), ((), ())), preferred_element_type=F32)


def gather_kernel(
    state_hbm,
    ms_hbm,
    stiff_hbm,
    face_hbm,
    deriv_hbm,
    volume_ref,
    amp_ref,
    owner_ref,
    links_ref,
    res_ref,
    xraw,
    xflat,
    x,
    st_in,
    ms_own,
    ms_oth,
    snd_own,
    snd_oth,
    ms_in,
    ret_out,
    ret_in,
    amp_out,
    amp_in,
    fcv,
    stv,
    dv,
    sel,
    placing,
    forcing,
    local_sem,
    st_ssem,
    st_rsem,
    rt_ssem,
    rt_rsem,
    ms_ssem,
    ms_rsem,
    am_ssem,
    am_rsem,
    halo_ssem,
    halo_rsem,
):
    inst = lax.axis_index("inst")
    slab = lax.axis_index("slab")
    zz, yl = inst // 2, inst % 2
    yh, mine = slab // 8, slab % 8
    inst_oth = zz * 2 + (1 - yl)

    def local(src, dst, k):
        return pltpu.make_async_copy(src, dst, local_sem.at[k])

    state_cp = local(state_hbm, xraw.at[pl.ds(0, NB)], 0)
    state_cp.start()

    def ms_head(dst, grp, k):
        return local(ms_hbm.at[pl.ds(grp * GRP, LAST)], dst.at[pl.ds(0, LAST)], k)

    def ms_tail(dst, grp, k):
        return local(
            ms_hbm.at[pl.ds(grp * GRP + LAST, GRP - LAST)], dst.at[pl.ds(LAST, GRP - LAST)], k
        )

    for dst, grp, k in ((ms_own, inst, 1), (ms_oth, inst_oth, 3)):
        ms_head(dst, grp, k).start()

        @pl.when(grp < 7)
        def _():
            ms_tail(dst, grp, k + 1).start()

        @pl.when(grp == 7)
        def _():
            dst[LAST:GRP] = jnp.zeros((GRP - LAST, 8, NE), BF16)

    stiff_cp = local(stiff_hbm, stv, 5)
    stiff_cp.start()
    deriv_cp = local(deriv_hbm, dv, 6)
    deriv_cp.start()
    face_cp = local(face_hbm, fcv, 7)
    face_cp.start()

    def peer(d):
        return ((zz + d // 2) % 4) * 2 + (yl + d % 2) % 2

    order = (4, 5, 2, 6, 3, 7, 1)
    barrier = pltpu.get_barrier_semaphore()

    def greet(i, s):
        pl.semaphore_signal(barrier, inc=1, device_id={"inst": i, "slab": s}, device_id_type=MESH)

    for d in order:
        greet(peer(d), slab)
    for d in range(1, 8):
        greet(inst, yh * 8 + (mine + d) % 8)
    for d in range(8):
        greet(inst_oth, (1 - yh) * 8 + (mine + d) % 8)
    greet(inst, 15 - slab)

    lane8 = lax.broadcasted_iota(jnp.int32, (8, 128), 1)
    row8 = lax.broadcasted_iota(jnp.int32, (8, 128), 0)
    tiled = jnp.zeros((8, 128), F32)
    amp = amp_ref[...]
    for j in range(2):
        for k in range(8):
            tiled = jnp.where((row8 == j) & (lane8 % 8 == k), amp[j : j + 1, k : k + 1], tiled)
    amp_out[...] = tiled
    amp_in[inst] = tiled

    state_cp.wait()
    xraw[NB:NBP] = jnp.zeros((NBP - NB, 8, 128), BF16)

    def split(g, carry):
        rows = xraw[pl.ds(g * GRP, GRP)].astype(F32).reshape(GRP * 8, 128)
        xflat[...] = rows
        for i in range(2):
            for c in range(4):
                part = xflat[pl.ds(c * 2 + i, GRP, stride=8), :]
                x[i, pl.ds(pl.multiple_of(g * GRP, 16), GRP), c * 128 : (c + 1) * 128] = part.astype(BF16)
        return carry

    lax.fori_loop(0, 8, split, 0)

    @pl.when(slab == 0)
    def _():
        x[:, :, 512:640] = jnp.zeros((2, NBP, 128), BF16)

    @pl.when(slab == 15)
    def _():
        x[:, :, 640:768] = jnp.zeros((2, NBP, 128), BF16)

    for i in range(2):
        st_in[inst, i] = x[i, pl.ds(pl.multiple_of(inst * GRP, 16), GRP), 0:NE]

    pl.semaphore_wait(barrier, 23)

    def state_copy(h, d):
        start, size = HALVES[h]
        p = peer(d)
        return pltpu.make_async_remote_copy(
            src_ref=x.at[:, pl.ds(pl.multiple_of(p * GRP + start, 16), size), pl.ds(0, NE)],
            dst_ref=st_in.at[inst, :, pl.ds(start, size), :],
            send_sem=st_ssem.at[h, d],
            recv_sem=st_rsem.at[h, d],
            device_id={"inst": p, "slab": slab},
            device_id_type=MESH,
        )

    def amp_copy(d):
        return pltpu.make_async_remote_copy(
            src_ref=amp_out,
            dst_ref=amp_in.at[inst],
            send_sem=am_ssem.at[d],
            recv_sem=am_rsem.at[d],
            device_id={"inst": peer(d), "slab": slab},
            device_id_type=MESH,
        )

    def halo_copy(k):
        src, dst, to = ((384, 512, slab + 1), (0, 640, slab - 1))[k]
        return pltpu.make_async_remote_copy(
            src_ref=x.at[:, :, pl.ds(src, 128)],
            dst_ref=x.at[:, :, pl.ds(dst, 128)],
            send_sem=halo_ssem.at[k],
            recv_sem=halo_rsem.at[k],
            device_id={"inst": inst, "slab": to},
            device_id_type=MESH,
        )

    for d in order:
        amp_copy(d).start()
    for d in order:
        state_copy(0, d).start()

    @pl.when(slab < 15)
    def _():
        halo_copy(0).start()

    @pl.when(slab > 0)
    def _():
        halo_copy(1).start()

    for d in order:
        state_copy(1, d).start()

    own = jnp.concatenate([owner_ref[pl.ds(c, 16, stride=4), :] for c in range(4)], axis=1)
    target = own // NE
    element = own - target * NE
    row16 = lax.broadcasted_iota(jnp.int32, (16, NE), 0)
    my_target = jnp.sum(jnp.where(row16 == slab, target, 0), axis=0, keepdims=True)
    up_r = lax.broadcasted_iota(jnp.int32, (NE, NE), 0)
    up_c = lax.broadcasted_iota(jnp.int32, (NE, NE), 1)
    upper = jnp.where(up_r < up_c, 1.0, 0.0).astype(BF16)
    match = jnp.where(row16 == my_target, 1.0, 0.0)
    before = dot(match.astype(BF16), upper)
    rank = jnp.sum(match * before, axis=0, keepdims=True)
    slot = my_target * 32 + rank.astype(jnp.int32)
    s_iota = lax.broadcasted_iota(jnp.int32, (256, NE), 0)
    pick_own = jnp.where(s_iota + yh * 256 == slot, 1.0, 0.0).astype(BF16)
    pick_oth = jnp.where(s_iota + (1 - yh) * 256 == slot, 1.0, 0.0).astype(BF16)

    for dst, grp, k in ((ms_own, inst, 1), (ms_oth, inst_oth, 3)):
        ms_head(dst, grp, k).wait()

        @pl.when(grp < 7)
        def _():
            ms_tail(dst, grp, k + 1).wait()

    snd_own[...] = dot_nt(pick_own, ms_own[...].astype(F32).reshape(GRP * 8, NE).astype(BF16)).astype(BF16)
    snd_oth[...] = dot_nt(pick_oth, ms_oth[...].astype(F32).reshape(GRP * 8, NE).astype(BF16)).astype(BF16)

    def ms_copy(d, other):
        idx = (mine + d) % 8
        src = snd_oth if other else snd_own
        return pltpu.make_async_remote_copy(
            src_ref=src.at[pl.ds(pl.multiple_of(idx * 32, 32), 32), :],
            dst_ref=ms_in.at[pl.ds(pl.multiple_of(slab * 32, 32), 32), :],
            send_sem=ms_ssem.at[int(other), d],
            recv_sem=ms_rsem.at[int(other), d],
            device_id={
                "inst": inst_oth if other else inst,
                "slab": ((1 - yh) if other else yh) * 8 + idx,
            },
            device_id_type=MESH,
        )

    for d in range(8):
        ms_copy(d, True).start()
    for d in range(1, 8):
        ms_copy(d, False).start()
    ms_self = local(
        snd_own.at[pl.ds(pl.multiple_of(mine * 32, 32), 32), :],
        ms_in.at[pl.ds(pl.multiple_of(slab * 32, 32), 32), :],
        8,
    )
    ms_self.start()

    hits = jnp.where(target == slab, 1.0, 0.0)
    ranks = dot(hits.astype(BF16), upper)
    ranks = jnp.where(hits > 0.5, ranks, -1.0)
    element_f = element.astype(F32)
    c_iota = lax.broadcasted_iota(jnp.int32, (32, NE), 0).astype(F32)
    e_iota = lax.broadcasted_iota(jnp.int32, (32, NE), 1).astype(F32)
    for s in range(16):
        found = jnp.where(ranks[s : s + 1, :] == c_iota, element_f[s : s + 1, :], 0.0)
        column = jnp.sum(found, axis=1, keepdims=True)
        placing[32 * s : 32 * s + 32, :] = jnp.where(column == e_iota, 1.0, 0.0).astype(BF16)

    links = links_ref[...]
    where_to = jnp.where(links < 64, links + 576, jnp.where(links < 576, links - 64, links + 64))

    def face(f):
        span = lax.broadcasted_iota(jnp.int32, (768, NE), 0)
        sel[...] = jnp.where(span == where_to[f : f + 1, :], 1.0, 0.0).astype(BF16)
        for i in range(2):
            picked = dot(x[i], sel[...]).astype(BF16)
            res_ref[i, 0:NB] += dot(fcv[f], picked[0:NB])

    stiff_cp.wait()
    for i in range(2):
        res_ref[i, 0:NB] = dot(stv[...], x[i, 0:NB, 0:NE])

    for d in order:
        amp_copy(d).wait_recv()
    a_all = jnp.concatenate([amp_in[p, 0:2] for p in range(8)], axis=0)
    a_all = jnp.broadcast_to(a_all[:, None, :], (16, 16, 128)).reshape(256, 128)
    k_row = lax.broadcasted_iota(jnp.int32, (256, 128), 0) % 16
    k_col = lax.broadcasted_iota(jnp.int32, (256, 128), 1) // 8
    a_all = jnp.where(k_row == k_col, a_all, 0.0)
    a_high = a_all.astype(BF16)
    a_low = (a_all - a_high.astype(F32)).astype(BF16)
    a_both = jnp.concatenate([a_high, a_low], axis=1)

    ms_self.wait()
    for d in range(8):
        ms_copy(d, True).wait_recv()
    for d in range(1, 8):
        ms_copy(d, False).wait_recv()
    for q in range(5):
        rows = ms_in[:, 128 * q : 128 * q + 128]
        deflection = dot_nt(a_both, jnp.concatenate([rows, rows], axis=1)).astype(BF16)
        forcing[q] = dot(deflection, placing[...])

    face_cp.wait()

    @pl.when(slab > 0)
    def _():
        halo_copy(0).wait_recv()

    @pl.when(slab < 15)
    def _():
        halo_copy(1).wait_recv()

    for f in range(FIRST_FACES):
        face(f)

    deriv_cp.wait()
    volume = jnp.concatenate([volume_ref[c : c + 1, :] for c in range(4)], axis=1)

    def ret_copy(h, d):
        start, size = HALVES[h]
        p = peer(d)
        return pltpu.make_async_remote_copy(
            src_ref=ret_out.at[p, :, pl.ds(start, size), :],
            dst_ref=ret_in.at[inst, :, pl.ds(start, size), :],
            send_sem=rt_ssem.at[h, d],
            recv_sem=rt_rsem.at[h, d],
            device_id={"inst": p, "slab": slab},
            device_id_type=MESH,
        )

    for h in range(2):
        for d in order:
            state_copy(h, d).wait_recv()
        start, size = HALVES[h]
        for q in range(start // 16, (start + size) // 16):
            block = st_in[:, :, 16 * q : 16 * q + 16, :].reshape(256, NE)
            spectral = dot(dv[0], block) + dot(dv[1], block)
            back = (volume * spectral - forcing[q]).astype(BF16)
            ret_out[:, :, 16 * q : 16 * q + 16, :] = back.reshape(8, 2, 16, NE)
        for d in order:
            ret_copy(h, d).start()

    for i in range(2):
        ret_in[inst, i] = ret_out[inst, i]

    for f in range(FIRST_FACES, 6):
        face(f)

    for h in range(2):
        for d in order:
            ret_copy(h, d).wait_recv()
    for i in range(2):
        for g in range(8):
            res_ref[i, g * GRP : (g + 1) * GRP] += ret_in[g, i].astype(F32)

    for d in order:
        amp_copy(d).wait_send()
        for h in range(2):
            state_copy(h, d).wait_send()
            ret_copy(h, d).wait_send()
    for d in range(8):
        ms_copy(d, True).wait_send()
    for d in range(1, 8):
        ms_copy(d, False).wait_send()

    @pl.when(slab < 15)
    def _():
        halo_copy(0).wait_send()

    @pl.when(slab > 0)
    def _():
        halo_copy(1).wait_send()


BLK = 128


def update_kernel(res_ref, state_ref, step_ref, precond_ref, res_out, new_out, rounded):
    j = pl.program_id(0)

    @pl.when(j == 0)
    def _():
        rounded[...] = res_ref[...].astype(BF16)

    base = pl.multiple_of(j * BLK, BLK)
    for i in range(2):
        change = dot(precond_ref[...], rounded[i, 0:NB])
        for c in range(4):
            lanes = slice(c * 128, (c + 1) * 128)
            rows = pl.ds(c * 2 + i, BLK, stride=8)
            res_out[rows, :] = res_ref[i, pl.ds(base, BLK), lanes]
            new_out[rows, :] = step_ref[c : c + 1, :] * change[:, lanes]
    new_out[...] = state_ref[...].astype(F32).reshape(BLK * 8, 128) - new_out[...]


def body(state, volume, step_size, stiffness, face_coupling, precond, mode_shapes, amplitudes, surface_owner, face_links):
    raw = state.reshape(2, NB, 4, 128).transpose(1, 2, 0, 3).reshape(NB, 8, 128)
    shapes = mode_shapes.transpose(1, 0, 2)
    any_spec = pl.BlockSpec(memory_space=pl.ANY)
    vmem = pl.BlockSpec(memory_space=pltpu.VMEM)
    dma = pltpu.SemaphoreType.DMA
    res = pl.pallas_call(
        gather_kernel,
        out_shape=jax.ShapeDtypeStruct((2, NBP, NE), F32),
        in_specs=[any_spec] * 5 + [vmem] * 4,
        out_specs=vmem,
        scratch_shapes=[
            pltpu.VMEM((NBP, 8, 128), BF16),
            pltpu.VMEM((GRP * 8, 128), F32),
            pltpu.VMEM((2, NBP, 768), BF16),
            pltpu.VMEM((8, 2, GRP, NE), BF16),
            pltpu.VMEM((GRP, 8, NE), BF16),
            pltpu.VMEM((GRP, 8, NE), BF16),
            pltpu.VMEM((256, GRP * 8), BF16),
            pltpu.VMEM((256, GRP * 8), BF16),
            pltpu.VMEM((512, GRP * 8), BF16),
            pltpu.VMEM((8, 2, GRP, NE), BF16),
            pltpu.VMEM((8, 2, GRP, NE), BF16),
            pltpu.VMEM((8, 128), F32),
            pltpu.VMEM((8, 8, 128), F32),
            pltpu.VMEM((6, NB, NB), BF16),
            pltpu.VMEM((NB, NB), BF16),
            pltpu.VMEM((2, 256, 256), BF16),
            pltpu.VMEM((768, NE), BF16),
            pltpu.VMEM((512, NE), BF16),
            pltpu.VMEM((5, 256, NE), F32),
            dma((9,)),
            dma((2, 8)),
            dma((2, 8)),
            dma((2, 8)),
            dma((2, 8)),
            dma((2, 8)),
            dma((2, 8)),
            dma((8,)),
            dma((8,)),
            dma((2,)),
            dma((2,)),
        ],
        compiler_params=pltpu.CompilerParams(
            collective_id=0, has_side_effects=True, vmem_limit_bytes=56 << 20
        ),
        cost_estimate=pl.CostEstimate(flops=13_000_000_000, bytes_accessed=16_000_000, transcendentals=0),
    )(
        raw,
        shapes,
        stiffness,
        face_coupling,
        jnp.asarray(derivative_blocks()),
        volume.reshape(4, 128),
        amplitudes,
        surface_owner.reshape(64, 128),
        face_links,
    )
    steps = pl.cdiv(NB, BLK)
    res_raw, new_raw = pl.pallas_call(
        update_kernel,
        grid=(steps,),
        out_shape=[jax.ShapeDtypeStruct((NB * 8, 128), F32)] * 2,
        in_specs=[
            pl.BlockSpec((2, NBP, NE), lambda j: (0, 0, 0)),
            pl.BlockSpec((BLK, 8, 128), lambda j: (j, 0, 0)),
            pl.BlockSpec((4, 128), lambda j: (0, 0)),
            pl.BlockSpec((BLK, NB), lambda j: (j, 0)),
        ],
        out_specs=[pl.BlockSpec((BLK * 8, 128), lambda j: (j, 0))] * 2,
        scratch_shapes=[pltpu.VMEM((2, NBP, NE), BF16)],
        compiler_params=pltpu.CompilerParams(vmem_limit_bytes=40 << 20),
        cost_estimate=pl.CostEstimate(flops=800_000_000, bytes_accessed=10_000_000, transcendentals=0),
    )(res, raw, step_size.reshape(4, 128), precond)

    def whole(a):
        return a.reshape(NB, 4, 2, 128).transpose(2, 0, 1, 3).reshape(2, NB, NE)

    return whole(res_raw), whole(new_raw)


def solution(mesh):
    return jax.shard_map(
        body,
        mesh=mesh,
        in_specs=(
            P("inst", None, "slab"),
            P("slab"),
            P("slab"),
            P(),
            P(),
            P(),
            P(None, None, "slab"),
            P("inst", None),
            P(),
            P(None, "slab"),
        ),
        out_specs=(P("inst", None, "slab"), P("inst", None, "slab")),
        check_vma=False,
    )
```

profile of v0, /device:TPU:1, one launch (start us, length us, event | category | flops | bytes accessed | tf_op | source)
XLA Modules:
  0.0 57.5 jit_solution(15395639748016352093)
XLA Ops:
  0.6 0.0 copy-start.1
  0.6 0.0 copy-start.2
  0.7 0.0 copy-start.3
  0.7 50.6 %shard_map.122.res_ref = f32[2,640,512]{2,1,0:T(8,128)} custom-call(bf16[625,8,128]{2,1,0:T(8,128)(2,1)} %bitcast.19, bf16[625,8,512]{2,1,0:T(8,128)(2,1)} %bitcast.22, bf16[625,625]{1,0:T(8,128)(2,1)} %stiff_hbm.1, bf16[6,625,625]{2,1,0:T(8,128)(2,1)} %face_hbm.1, bf16[2,256,256]{2,1,0:T(8,128)(2,1)} %constant.2.clone.deriv_hbm, f32[4,128]{1,0:T(4,128)} %bitcast.26, ...), custom_call_target="tpu_custom_call" | custom-call | flops 12999999488 | bytes 16000000 | tf_op jit(solution)/shard_map/pallas_call | solution.py:422
  51.2 0.0 copy-done.1
  51.3 0.0 copy-done.2
  51.3 0.0 copy-done.3
  51.3 0.0 copy-start
  51.3 1.7 %copy-done = f32[2,640,512]{2,1,0:T(8,128)S(1)} copy-done((f32[2,640,512]{2,1,0:T(8,128)S(1)}, f32[2,640,512]{2,1,0:T(8,128)}, u32[]{:S(2)}) %copy-start) | copy-done | bytes 2621464
  53.0 4.4 %shard_map.123 = (f32[5000,128]{1,0:T(8,128)}, f32[5000,128]{1,0:T(8,128)}) custom-call(f32[2,640,512]{2,1,0:T(8,128)S(1)} %copy-done, bf16[625,8,128]{2,1,0:T(8,128)(2,1)S(1)} %bitcast.20, f32[4,128]{1,0:T(4,128)S(1)} %bitcast.21, bf16[625,625]{1,0:T(8,128)(2,1)S(1)} %copy-done.2), custom_call_target="tpu_custom_call" | custom-call | flops 800000000 | bytes 10000000 | tf_op jit(solution)/shard_map/pallas_call | solution.py:475
Async XLA Ops:
  0.6 50.6 %copy-start.1 = (bf16[2,625,512]{2,0,1:T(2,128)(2,1)S(1)}, bf16[2,625,512]{2,0,1:T(2,128)(2,1)}, u32[]{:S(2)}) copy-start(bf16[2,625,512]{2,0,1:T(2,128)(2,1)} %param.11) | copy-start | bytes 3840004
  0.6 50.6 %copy-start.2 = (bf16[625,625]{1,0:T(8,128)(2,1)S(1)}, bf16[625,625]{1,0:T(8,128)(2,1)}, u32[]{:S(2)}) copy-start(bf16[625,625]{1,0:T(8,128)(2,1)} %precond_ref.1) | copy-start | bytes 2343754
  0.7 50.6 %copy-start.3 = (f32[512]{0:T(512)S(1)}, f32[512]{0:T(512)}, u32[]{:S(2)}) copy-start(f32[512]{0:T(512)} %param.13) | copy-start | bytes 6148
  51.3 1.7 %copy-start = (f32[2,640,512]{2,1,0:T(8,128)S(1)}, f32[2,640,512]{2,1,0:T(8,128)}, u32[]{:S(2)}) copy-start(f32[2,640,512]{2,1,0:T(8,128)} %shard_map.122.res_ref) | copy-start | bytes 7864324
where the time goes:
time: 57.6 us; the launch traced here: 57.5 us
  Pallas kernels  55 us (95%)
  local copies, waits for them, and re-layouts  1.75 us (3%)
  between operations  0.7 us (1%)
    pallas_call x1, Pallas kernels, body(): pl.pallas_call(gather_kernel, out_shape=jax.ShapeDtypeStruct((2, NBP, NE)...  50.6 us
    pallas_call x1, Pallas kernels, body(): pl.pallas_call(update_kernel, grid=(steps,), out_shape=[jax.ShapeDtypeStr...  4.45 us
    unnamed x8, local copies, waits for them, and re-layouts  1.75 us

commit v1 on v0

--- a/solution.py
+++ b/solution.py
@@ -17,7 +17,7 @@
 LAST = NB - 7 * GRP
 NE = 512
 HALVES = ((0, 48), (48, 32))
-FIRST_FACES = 3
+FIRST_FACES = 1
 
 
 def derivative_blocks():
@@ -44,12 +44,18 @@
     ms_hbm,
     stiff_hbm,
     face_hbm,
+    precond_hbm,
     deriv_hbm,
     volume_ref,
+    step_ref,
     amp_ref,
     owner_ref,
     links_ref,
     res_ref,
+    new_ref,
+    acc,
+    rounded,
+    pcv,
     xraw,
     xflat,
     x,
@@ -118,6 +124,8 @@
     deriv_cp.start()
     face_cp = local(face_hbm, fcv, 7)
     face_cp.start()
+    precond_cp = local(precond_hbm, pcv, 9)
+    precond_cp.start()
 
     def peer(d):
         return ((zz + d // 2) % 4) * 2 + (yl + d % 2) % 2
@@ -171,7 +179,6 @@
     for i in range(2):
         st_in[inst, i] = x[i, pl.ds(pl.multiple_of(inst * GRP, 16), GRP), 0:NE]
 
-    pl.semaphore_wait(barrier, 23)
 
     def state_copy(h, d):
         start, size = HALVES[h]
@@ -205,22 +212,6 @@
             device_id={"inst": inst, "slab": to},
             device_id_type=MESH,
         )
-
-    for d in order:
-        amp_copy(d).start()
-    for d in order:
-        state_copy(0, d).start()
-
-    @pl.when(slab < 15)
-    def _():
-        halo_copy(0).start()
-
-    @pl.when(slab > 0)
-    def _():
-        halo_copy(1).start()
-
-    for d in order:
-        state_copy(1, d).start()
 
     own = jnp.concatenate([owner_ref[pl.ds(c, 16, stride=4), :] for c in range(4)], axis=1)
     target = own // NE
@@ -263,10 +254,26 @@
             device_id_type=MESH,
         )
 
+    pl.semaphore_wait(barrier, 23)
+    for d in order:
+        amp_copy(d).start()
+    for d in order:
+        state_copy(0, d).start()
+
+    @pl.when(slab < 15)
+    def _():
+        halo_copy(0).start()
+
+    @pl.when(slab > 0)
+    def _():
+        halo_copy(1).start()
+
     for d in range(8):
         ms_copy(d, True).start()
     for d in range(1, 8):
         ms_copy(d, False).start()
+    for d in order:
+        state_copy(1, d).start()
     ms_self = local(
         snd_own.at[pl.ds(pl.multiple_of(mine * 32, 32), 32), :],
         ms_in.at[pl.ds(pl.multiple_of(slab * 32, 32), 32), :],
@@ -293,11 +300,11 @@
         sel[...] = jnp.where(span == where_to[f : f + 1, :], 1.0, 0.0).astype(BF16)
         for i in range(2):
             picked = dot(x[i], sel[...]).astype(BF16)
-            res_ref[i, 0:NB] += dot(fcv[f], picked[0:NB])
+            acc[i, 0:NB] += dot(fcv[f], picked[0:NB])
 
     stiff_cp.wait()
     for i in range(2):
-        res_ref[i, 0:NB] = dot(stv[...], x[i, 0:NB, 0:NE])
+        acc[i, 0:NB] = dot(stv[...], x[i, 0:NB, 0:NE])
 
     for d in order:
         amp_copy(d).wait_recv()
@@ -369,9 +376,22 @@
     for h in range(2):
         for d in order:
             ret_copy(h, d).wait_recv()
+    precond_cp.wait()
     for i in range(2):
         for g in range(8):
-            res_ref[i, g * GRP : (g + 1) * GRP] += ret_in[g, i].astype(F32)
+            total = acc[i, g * GRP : (g + 1) * GRP] + ret_in[g, i].astype(F32)
+            rounded[i, g * GRP : (g + 1) * GRP] = total.astype(BF16)
+            count = GRP if g < 7 else LAST
+            for c in range(4):
+                res_ref[pl.ds(g * GRP * 8 + c * 2 + i, count, stride=8), :] = total[
+                    0:count, c * 128 : (c + 1) * 128
+                ]
+    for i in range(2):
+        change = dot(pcv[...], rounded[i, 0:NB])
+        for c in range(4):
+            lanes = slice(c * 128, (c + 1) * 128)
+            new = x[i, 0:NB, lanes].astype(F32) - step_ref[c : c + 1, :] * change[:, lanes]
+            new_ref[pl.ds(c * 2 + i, NB, stride=8), :] = new
 
     for d in order:
         amp_copy(d).wait_send()
@@ -392,39 +412,21 @@
         halo_copy(1).wait_send()
 
 
-BLK = 128
-
-
-def update_kernel(res_ref, state_ref, step_ref, precond_ref, res_out, new_out, rounded):
-    j = pl.program_id(0)
-
-    @pl.when(j == 0)
-    def _():
-        rounded[...] = res_ref[...].astype(BF16)
-
-    base = pl.multiple_of(j * BLK, BLK)
-    for i in range(2):
-        change = dot(precond_ref[...], rounded[i, 0:NB])
-        for c in range(4):
-            lanes = slice(c * 128, (c + 1) * 128)
-            rows = pl.ds(c * 2 + i, BLK, stride=8)
-            res_out[rows, :] = res_ref[i, pl.ds(base, BLK), lanes]
-            new_out[rows, :] = step_ref[c : c + 1, :] * change[:, lanes]
-    new_out[...] = state_ref[...].astype(F32).reshape(BLK * 8, 128) - new_out[...]
-
-
 def body(state, volume, step_size, stiffness, face_coupling, precond, mode_shapes, amplitudes, surface_owner, face_links):
     raw = state.reshape(2, NB, 4, 128).transpose(1, 2, 0, 3).reshape(NB, 8, 128)
     shapes = mode_shapes.transpose(1, 0, 2)
     any_spec = pl.BlockSpec(memory_space=pl.ANY)
     vmem = pl.BlockSpec(memory_space=pltpu.VMEM)
     dma = pltpu.SemaphoreType.DMA
-    res = pl.pallas_call(
+    res_raw, new_raw = pl.pallas_call(
         gather_kernel,
-        out_shape=jax.ShapeDtypeStruct((2, NBP, NE), F32),
-        in_specs=[any_spec] * 5 + [vmem] * 4,
-        out_specs=vmem,
+        out_shape=[pltpu.VMEM((NB * 8, 128), F32)] * 2,
+        in_specs=[any_spec] * 6 + [vmem] * 5,
+        out_specs=[vmem] * 2,
         scratch_shapes=[
+            pltpu.VMEM((2, NBP, NE), F32),
+            pltpu.VMEM((2, NBP, NE), BF16),
+            pltpu.VMEM((NB, NB), BF16),
             pltpu.VMEM((NBP, 8, 128), BF16),
             pltpu.VMEM((GRP * 8, 128), F32),
             pltpu.VMEM((2, NBP, 768), BF16),
@@ -444,7 +446,7 @@
             pltpu.VMEM((768, NE), BF16),
             pltpu.VMEM((512, NE), BF16),
             pltpu.VMEM((5, 256, NE), F32),
-            dma((9,)),
+            dma((10,)),
             dma((2, 8)),
             dma((2, 8)),
             dma((2, 8)),
@@ -465,29 +467,14 @@
         shapes,
         stiffness,
         face_coupling,
+        precond,
         jnp.asarray(derivative_blocks()),
         volume.reshape(4, 128),
+        step_size.reshape(4, 128),
         amplitudes,
         surface_owner.reshape(64, 128),
         face_links,
     )
-    steps = pl.cdiv(NB, BLK)
-    res_raw, new_raw = pl.pallas_call(
-        update_kernel,
-        grid=(steps,),
-        out_shape=[jax.ShapeDtypeStruct((NB * 8, 128), F32)] * 2,
-        in_specs=[
-            pl.BlockSpec((2, NBP, NE), lambda j: (0, 0, 0)),
-            pl.BlockSpec((BLK, 8, 128), lambda j: (j, 0, 0)),
-            pl.BlockSpec((4, 128), lambda j: (0, 0)),
-            pl.BlockSpec((BLK, NB), lambda j: (j, 0)),
-        ],
-        out_specs=[pl.BlockSpec((BLK * 8, 128), lambda j: (j, 0))] * 2,
-        scratch_shapes=[pltpu.VMEM((2, NBP, NE), BF16)],
-        compiler_params=pltpu.CompilerParams(vmem_limit_bytes=40 << 20),
-        cost_estimate=pl.CostEstimate(flops=800_000_000, bytes_accessed=10_000_000, transcendentals=0),
-    )(res, raw, step_size.reshape(4, 128), precond)
-
     def whole(a):
         return a.reshape(NB, 4, 2, 128).transpose(2, 0, 1, 3).reshape(2, NB, NE)
 

time: 57.6 us -> 49.8 us (0.86)
  Pallas kernels: 55 us -> 46.1 us
  local copies, waits for them, and re-layouts: 1.75 us -> 2.95 us
    pallas_call x2 -> x1, Pallas kernels: 55 us -> 46.1 us  [body(): pl.pallas_call(gather_kernel, out_shape=[pltpu.VMEM((NB * 8, 128), F32)]...]
    unnamed x8 -> x2, local copies, waits for them, and re-layouts: 1.75 us -> 2.95 us
where the time goes in v1:
time: 49.8 us; the launch traced here: 49.7 us
  Pallas kernels  46.1 us (93%)
  local copies, waits for them, and re-layouts  2.95 us (6%)
  between operations  0.64 us (1%)
    pallas_call x1, Pallas kernels, body(): pl.pallas_call(gather_kernel, out_shape=[pltpu.VMEM((NB * 8, 128), F32)]...  46.1 us
    unnamed x2, local copies, waits for them, and re-layouts  2.95 us

profile of v1, /device:TPU:1, one launch (start us, length us, event | category | flops | bytes accessed | tf_op | source)
XLA Modules:
  0.0 49.7 jit_solution(10339376816192844722)
XLA Ops:
  0.6 46.1 %shard_map.122 = (f32[5000,128]{1,0:T(8,128)S(1)}, f32[5000,128]{1,0:T(8,128)S(1)}) custom-call(bf16[625,8,128]{2,1,0:T(8,128)(2,1)} %bitcast.22, bf16[625,8,512]{2,1,0:T(8,128)(2,1)} %bitcast.21, bf16[625,625]{1,0:T(8,128)(2,1)} %stiff_hbm.1, bf16[6,625,625]{2,1,0:T(8,128)(2,1)} %face_hbm.1, bf16[625,625]{1,0:T(8,128)(2,1)} %precond_hbm.1, ...), custom_call_target="tpu_custom_call" | custom-call | flops 12999999488 | bytes 16000000 | tf_op jit(solution)/shard_map/pallas_call | solution.py:421
  46.7 1.5 %copy.18 = f32[2,625,512]{2,0,1:T(2,128)} copy(f32[2,625,512]{2,0,1:T(2,128)S(1)} %bitcast.20) | data formatting | bytes 5120000
  48.2 1.5 %copy.19 = f32[2,625,512]{2,0,1:T(2,128)} copy(f32[2,625,512]{2,0,1:T(2,128)S(1)} %bitcast.19) | data formatting | bytes 5120000

commit v2 on v1

--- a/solution.py
+++ b/solution.py
@@ -16,8 +16,10 @@
 GRP = 80
 LAST = NB - 7 * GRP
 NE = 512
-HALVES = ((0, 48), (48, 32))
-FIRST_FACES = 1
+PIECES = ((0, 48), (48, 32))
+TAIL = ((0, 48), (48, 32))
+FIRST_PIECES = 1
+PLAN = (0, 4, 8)
 
 
 def derivative_blocks():
@@ -46,19 +48,28 @@
     face_hbm,
     precond_hbm,
     deriv_hbm,
+    volume_hbm,
+    step_hbm,
+    amp_hbm,
+    owner_hbm,
+    links_hbm,
+    res_ref,
+    new_ref,
     volume_ref,
     step_ref,
     amp_ref,
     owner_ref,
     links_ref,
-    res_ref,
-    new_ref,
     acc,
     rounded,
     pcv,
+    pc_cols,
+    change,
     xraw,
     xflat,
     x,
+    halo,
+    halo_out,
     st_in,
     ms_own,
     ms_oth,
@@ -107,6 +118,72 @@
             ms_hbm.at[pl.ds(grp * GRP + LAST, GRP - LAST)], dst.at[pl.ds(LAST, GRP - LAST)], k
         )
 
+    small = [
+        local(src, dst, 10 + k)
+        for k, (src, dst) in enumerate(
+            (
+                (amp_hbm, amp_ref),
+                (owner_hbm, owner_ref),
+                (links_hbm, links_ref),
+                (volume_hbm, volume_ref),
+                (step_hbm, step_ref),
+            )
+        )
+    ]
+
+    def peer(d):
+        return ((zz + d // 2) % 4) * 2 + (yl + d % 2) % 2
+
+    order = (4, 5, 2, 6, 3, 7, 1)
+    barrier = pltpu.get_barrier_semaphore()
+
+    def greet(i, s):
+        pl.semaphore_signal(barrier, inc=1, device_id={"inst": i, "slab": s}, device_id_type=MESH)
+
+    for d in order:
+        greet(peer(d), slab)
+    for d in range(1, 8):
+        greet(inst, yh * 8 + (mine + d) % 8)
+    for d in range(8):
+        greet(inst_oth, (1 - yh) * 8 + (mine + d) % 8)
+    greet(inst, 15 - slab)
+    for copy in small:
+        copy.start()
+
+    def state_copy(h, d):
+        start, size = PIECES[h]
+        p = peer(d)
+        return pltpu.make_async_remote_copy(
+            src_ref=x.at[:, pl.ds(pl.multiple_of(p * GRP + start, 16), size)],
+            dst_ref=st_in.at[inst, :, pl.ds(start, size), :],
+            send_sem=st_ssem.at[h, d],
+            recv_sem=st_rsem.at[h, d],
+            device_id={"inst": p, "slab": slab},
+            device_id_type=MESH,
+        )
+
+    def amp_copy(d):
+        return pltpu.make_async_remote_copy(
+            src_ref=amp_out,
+            dst_ref=amp_in.at[inst],
+            send_sem=am_ssem.at[d],
+            recv_sem=am_rsem.at[d],
+            device_id={"inst": peer(d), "slab": slab},
+            device_id_type=MESH,
+        )
+
+    def halo_copy(k):
+        dst, to = ((0, slab + 1), (128, slab - 1))[k]
+        return pltpu.make_async_remote_copy(
+            src_ref=halo_out.at[k],
+            dst_ref=halo.at[:, pl.ds(dst, 128)],
+            send_sem=halo_ssem.at[k],
+            recv_sem=halo_rsem.at[k],
+            device_id={"inst": inst, "slab": to},
+            device_id_type=MESH,
+        )
+
+    state_cp.wait()
     for dst, grp, k in ((ms_own, inst, 1), (ms_oth, inst_oth, 3)):
         ms_head(dst, grp, k).start()
 
@@ -117,7 +194,30 @@
         @pl.when(grp == 7)
         def _():
             dst[LAST:GRP] = jnp.zeros((GRP - LAST, 8, NE), BF16)
-
+    xraw[NB:NBP] = jnp.zeros((NBP - NB, 8, 128), BF16)
+
+    def split(g):
+        rows = xraw[pl.ds(g * GRP, GRP)].astype(F32).reshape(GRP * 8, 128)
+        xflat[...] = rows
+        parts = {}
+        for i in range(2):
+            for c in range(4):
+                part = xflat[pl.ds(c * 2 + i, GRP, stride=8), :]
+                x[i, pl.ds(pl.multiple_of(g * GRP, 16), GRP), c * 128 : (c + 1) * 128] = part.astype(BF16)
+                parts[c, i] = part
+        rows = pl.ds(pl.multiple_of(g * GRP, 16), GRP)
+        first = lax.broadcasted_iota(jnp.int32, (GRP, 128), 1) < 64
+        high = jnp.where(first, pltpu.roll(parts[3, 0], 64, 1), parts[3, 1])
+        low = jnp.where(first, parts[0, 0], pltpu.roll(parts[0, 1], 64, 1))
+        halo_out[0, rows, :] = high.astype(BF16)
+        halo_out[1, rows, :] = low.astype(BF16)
+
+    pl.semaphore_wait(barrier, 23)
+    for d in order:
+        split(peer(d))
+        for h in range(FIRST_PIECES):
+            state_copy(h, d).start()
+    split(inst)
     stiff_cp = local(stiff_hbm, stv, 5)
     stiff_cp.start()
     deriv_cp = local(deriv_hbm, dv, 6)
@@ -126,23 +226,20 @@
     face_cp.start()
     precond_cp = local(precond_hbm, pcv, 9)
     precond_cp.start()
-
-    def peer(d):
-        return ((zz + d // 2) % 4) * 2 + (yl + d % 2) % 2
-
-    order = (4, 5, 2, 6, 3, 7, 1)
-    barrier = pltpu.get_barrier_semaphore()
-
-    def greet(i, s):
-        pl.semaphore_signal(barrier, inc=1, device_id={"inst": i, "slab": s}, device_id_type=MESH)
-
-    for d in order:
-        greet(peer(d), slab)
-    for d in range(1, 8):
-        greet(inst, yh * 8 + (mine + d) % 8)
-    for d in range(8):
-        greet(inst_oth, (1 - yh) * 8 + (mine + d) % 8)
-    greet(inst, 15 - slab)
+    @pl.when(slab == 0)
+    def _():
+        halo[:, 0:128] = jnp.zeros((NBP, 128), BF16)
+
+    @pl.when(slab == 15)
+    def _():
+        halo[:, 128:256] = jnp.zeros((NBP, 128), BF16)
+
+    for i in range(2):
+        st_in[inst, i] = x[i, pl.ds(pl.multiple_of(inst * GRP, 16), GRP)]
+
+
+    for copy in small:
+        copy.wait()
 
     lane8 = lax.broadcasted_iota(jnp.int32, (8, 128), 1)
     row8 = lax.broadcasted_iota(jnp.int32, (8, 128), 0)
@@ -154,64 +251,8 @@
     amp_out[...] = tiled
     amp_in[inst] = tiled
 
-    state_cp.wait()
-    xraw[NB:NBP] = jnp.zeros((NBP - NB, 8, 128), BF16)
-
-    def split(g, carry):
-        rows = xraw[pl.ds(g * GRP, GRP)].astype(F32).reshape(GRP * 8, 128)
-        xflat[...] = rows
-        for i in range(2):
-            for c in range(4):
-                part = xflat[pl.ds(c * 2 + i, GRP, stride=8), :]
-                x[i, pl.ds(pl.multiple_of(g * GRP, 16), GRP), c * 128 : (c + 1) * 128] = part.astype(BF16)
-        return carry
-
-    lax.fori_loop(0, 8, split, 0)
-
-    @pl.when(slab == 0)
-    def _():
-        x[:, :, 512:640] = jnp.zeros((2, NBP, 128), BF16)
-
-    @pl.when(slab == 15)
-    def _():
-        x[:, :, 640:768] = jnp.zeros((2, NBP, 128), BF16)
-
-    for i in range(2):
-        st_in[inst, i] = x[i, pl.ds(pl.multiple_of(inst * GRP, 16), GRP), 0:NE]
-
-
-    def state_copy(h, d):
-        start, size = HALVES[h]
-        p = peer(d)
-        return pltpu.make_async_remote_copy(
-            src_ref=x.at[:, pl.ds(pl.multiple_of(p * GRP + start, 16), size), pl.ds(0, NE)],
-            dst_ref=st_in.at[inst, :, pl.ds(start, size), :],
-            send_sem=st_ssem.at[h, d],
-            recv_sem=st_rsem.at[h, d],
-            device_id={"inst": p, "slab": slab},
-            device_id_type=MESH,
-        )
-
-    def amp_copy(d):
-        return pltpu.make_async_remote_copy(
-            src_ref=amp_out,
-            dst_ref=amp_in.at[inst],
-            send_sem=am_ssem.at[d],
-            recv_sem=am_rsem.at[d],
-            device_id={"inst": peer(d), "slab": slab},
-            device_id_type=MESH,
-        )
-
-    def halo_copy(k):
-        src, dst, to = ((384, 512, slab + 1), (0, 640, slab - 1))[k]
-        return pltpu.make_async_remote_copy(
-            src_ref=x.at[:, :, pl.ds(src, 128)],
-            dst_ref=x.at[:, :, pl.ds(dst, 128)],
-            send_sem=halo_ssem.at[k],
-            recv_sem=halo_rsem.at[k],
-            device_id={"inst": inst, "slab": to},
-            device_id_type=MESH,
-        )
+    for d in order:
+        amp_copy(d).start()
 
     own = jnp.concatenate([owner_ref[pl.ds(c, 16, stride=4), :] for c in range(4)], axis=1)
     target = own // NE
@@ -254,12 +295,6 @@
             device_id_type=MESH,
         )
 
-    pl.semaphore_wait(barrier, 23)
-    for d in order:
-        amp_copy(d).start()
-    for d in order:
-        state_copy(0, d).start()
-
     @pl.when(slab < 15)
     def _():
         halo_copy(0).start()
@@ -272,8 +307,9 @@
         ms_copy(d, True).start()
     for d in range(1, 8):
         ms_copy(d, False).start()
-    for d in order:
-        state_copy(1, d).start()
+    for h in range(FIRST_PIECES, len(PIECES)):
+        for d in order:
+            state_copy(h, d).start()
     ms_self = local(
         snd_own.at[pl.ds(pl.multiple_of(mine * 32, 32), 32), :],
         ms_in.at[pl.ds(pl.multiple_of(slab * 32, 32), 32), :],
@@ -293,18 +329,22 @@
         placing[32 * s : 32 * s + 32, :] = jnp.where(column == e_iota, 1.0, 0.0).astype(BF16)
 
     links = links_ref[...]
-    where_to = jnp.where(links < 64, links + 576, jnp.where(links < 576, links - 64, links + 64))
-
-    def face(f):
-        span = lax.broadcasted_iota(jnp.int32, (768, NE), 0)
-        sel[...] = jnp.where(span == where_to[f : f + 1, :], 1.0, 0.0).astype(BF16)
-        for i in range(2):
-            picked = dot(x[i], sel[...]).astype(BF16)
-            acc[i, 0:NB] += dot(fcv[f], picked[0:NB])
-
+    inner = jnp.where((links >= 64) & (links < 576), links - 64, -1)
+    outer = jnp.where(links < 64, links, jnp.where(links < 576, -256, links - 448))
+
+    def half_face(u):
+        f, i = u // 2, u % 2
+        span = lax.broadcasted_iota(jnp.int32, (NE, NE), 0)
+        if i == 0:
+            sel[...] = jnp.where(span == inner[f : f + 1, :], 1.0, 0.0).astype(BF16)
+        edge = jnp.where(span[0:256] == outer[f : f + 1, :] + 64 * i, 1.0, 0.0).astype(BF16)
+        picked = (dot(x[i], sel[...]) + dot(halo[...], edge)).astype(BF16)
+        acc[i, 0:NB] += dot(fcv[f], picked[0:NB])
+
+    acc[:, NB:NBP] = jnp.zeros((2, NBP - NB, NE), F32)
     stiff_cp.wait()
     for i in range(2):
-        acc[i, 0:NB] = dot(stv[...], x[i, 0:NB, 0:NE])
+        acc[i, 0:NB] = dot(stv[...], x[i, 0:NB])
 
     for d in order:
         amp_copy(d).wait_recv()
@@ -337,14 +377,14 @@
     def _():
         halo_copy(1).wait_recv()
 
-    for f in range(FIRST_FACES):
-        face(f)
+    for u in range(PLAN[0]):
+        half_face(u)
 
     deriv_cp.wait()
     volume = jnp.concatenate([volume_ref[c : c + 1, :] for c in range(4)], axis=1)
 
     def ret_copy(h, d):
-        start, size = HALVES[h]
+        start, size = PIECES[h]
         p = peer(d)
         return pltpu.make_async_remote_copy(
             src_ref=ret_out.at[p, :, pl.ds(start, size), :],
@@ -355,10 +395,10 @@
             device_id_type=MESH,
         )
 
-    for h in range(2):
+    for h in range(len(PIECES)):
         for d in order:
             state_copy(h, d).wait_recv()
-        start, size = HALVES[h]
+        start, size = PIECES[h]
         for q in range(start // 16, (start + size) // 16):
             block = st_in[:, :, 16 * q : 16 * q + 16, :].reshape(256, NE)
             spectral = dot(dv[0], block) + dot(dv[1], block)
@@ -366,36 +406,54 @@
             ret_out[:, :, 16 * q : 16 * q + 16, :] = back.reshape(8, 2, 16, NE)
         for d in order:
             ret_copy(h, d).start()
+        if h == 0:
+            for u in range(PLAN[0], PLAN[0] + PLAN[1]):
+                half_face(u)
 
     for i in range(2):
         ret_in[inst, i] = ret_out[inst, i]
 
-    for f in range(FIRST_FACES, 6):
-        face(f)
+    for u in range(PLAN[0] + PLAN[1], 12):
+        half_face(u)
+
+    precond_cp.wait()
+    p_row = lax.broadcasted_iota(jnp.int32, (NB, NBP), 0)
+    p_col = lax.broadcasted_iota(jnp.int32, (NB, NBP), 1)
+    p_first = GRP * (p_col // 48) + p_col % 48
+    p_second = GRP * ((p_col - 384) // 32) + 48 + (p_col - 384) % 32
+    moved = jnp.where(p_row == jnp.where(p_col < 384, p_first, p_second), 1.0, 0.0).astype(BF16)
+    pc_cols[...] = dot(pcv[...], moved).astype(BF16)
 
     for h in range(2):
-        for d in order:
-            ret_copy(h, d).wait_recv()
-    precond_cp.wait()
-    for i in range(2):
-        for g in range(8):
-            total = acc[i, g * GRP : (g + 1) * GRP] + ret_in[g, i].astype(F32)
-            rounded[i, g * GRP : (g + 1) * GRP] = total.astype(BF16)
-            count = GRP if g < 7 else LAST
+        start, size = TAIL[h]
+        for k, (piece, _) in enumerate(PIECES):
+            if start <= piece < start + size:
+                for d in order:
+                    ret_copy(k, d).wait_recv()
+        base = 384 * h
+        for i in range(2):
+            for g in range(8):
+                row = g * GRP + start
+                total = acc[i, row : row + size] + ret_in[g, i, start : start + size].astype(F32)
+                rounded[i, base + g * size : base + (g + 1) * size] = total.astype(BF16)
+                count = min(size, NB - row)
+                for c in range(4):
+                    res_ref[pl.ds(row * 8 + c * 2 + i, count, stride=8), :] = total[
+                        0:count, c * 128 : (c + 1) * 128
+                    ]
+            part = dot(pc_cols[:, base : base + 8 * size], rounded[i, base : base + 8 * size])
+            if h == 0:
+                change[i] = part
+                continue
+            part = part + change[i]
             for c in range(4):
-                res_ref[pl.ds(g * GRP * 8 + c * 2 + i, count, stride=8), :] = total[
-                    0:count, c * 128 : (c + 1) * 128
-                ]
-    for i in range(2):
-        change = dot(pcv[...], rounded[i, 0:NB])
-        for c in range(4):
-            lanes = slice(c * 128, (c + 1) * 128)
-            new = x[i, 0:NB, lanes].astype(F32) - step_ref[c : c + 1, :] * change[:, lanes]
-            new_ref[pl.ds(c * 2 + i, NB, stride=8), :] = new
+                lanes = slice(c * 128, (c + 1) * 128)
+                new = x[i, 0:NB, lanes].astype(F32) - step_ref[c : c + 1, :] * part[:, lanes]
+                new_ref[pl.ds(c * 2 + i, NB, stride=8), :] = new
 
     for d in order:
         amp_copy(d).wait_send()
-        for h in range(2):
+        for h in range(len(PIECES)):
             state_copy(h, d).wait_send()
             ret_copy(h, d).wait_send()
     for d in range(8):
@@ -410,6 +468,17 @@
     @pl.when(slab > 0)
     def _():
         halo_copy(1).wait_send()
+
+
+def write_kernel(res_in, new_in, res_hbm, new_hbm, sem):
+    copies = [
+        pltpu.make_async_copy(res_in, res_hbm, sem.at[0]),
+        pltpu.make_async_copy(new_in, new_hbm, sem.at[1]),
+    ]
+    for copy in copies:
+        copy.start()
+    for copy in copies:
+        copy.wait()
 
 
 def body(state, volume, step_size, stiffness, face_coupling, precond, mode_shapes, amplitudes, surface_owner, face_links):
@@ -421,15 +490,24 @@
     res_raw, new_raw = pl.pallas_call(
         gather_kernel,
         out_shape=[pltpu.VMEM((NB * 8, 128), F32)] * 2,
-        in_specs=[any_spec] * 6 + [vmem] * 5,
+        in_specs=[any_spec] * 11,
         out_specs=[vmem] * 2,
         scratch_shapes=[
+            pltpu.VMEM((4, 128), F32),
+            pltpu.VMEM((4, 128), F32),
+            pltpu.VMEM((2, 8), F32),
+            pltpu.VMEM((64, 128), jnp.int32),
+            pltpu.VMEM((6, NE), jnp.int32),
             pltpu.VMEM((2, NBP, NE), F32),
             pltpu.VMEM((2, NBP, NE), BF16),
             pltpu.VMEM((NB, NB), BF16),
+            pltpu.VMEM((NB, NBP), BF16),
+            pltpu.VMEM((2, NB, NE), F32),
             pltpu.VMEM((NBP, 8, 128), BF16),
             pltpu.VMEM((GRP * 8, 128), F32),
-            pltpu.VMEM((2, NBP, 768), BF16),
+            pltpu.VMEM((2, NBP, NE), BF16),
+            pltpu.VMEM((NBP, 256), BF16),
+            pltpu.VMEM((2, NBP, 128), BF16),
             pltpu.VMEM((8, 2, GRP, NE), BF16),
             pltpu.VMEM((GRP, 8, NE), BF16),
             pltpu.VMEM((GRP, 8, NE), BF16),
@@ -443,14 +521,14 @@
             pltpu.VMEM((6, NB, NB), BF16),
             pltpu.VMEM((NB, NB), BF16),
             pltpu.VMEM((2, 256, 256), BF16),
-            pltpu.VMEM((768, NE), BF16),
+            pltpu.VMEM((NE, NE), BF16),
             pltpu.VMEM((512, NE), BF16),
             pltpu.VMEM((5, 256, NE), F32),
-            dma((10,)),
-            dma((2, 8)),
-            dma((2, 8)),
-            dma((2, 8)),
-            dma((2, 8)),
+            dma((15,)),
+            dma((len(PIECES), 8)),
+            dma((len(PIECES), 8)),
+            dma((len(PIECES), 8)),
+            dma((len(PIECES), 8)),
             dma((2, 8)),
             dma((2, 8)),
             dma((8,)),
@@ -475,6 +553,19 @@
         surface_owner.reshape(64, 128),
         face_links,
     )
+    res_raw, new_raw = pl.pallas_call(
+        write_kernel,
+        out_shape=[jax.ShapeDtypeStruct((NB * 8, 128), F32)] * 2,
+        in_specs=[vmem] * 2,
+        out_specs=[any_spec] * 2,
+        scratch_shapes=[dma((2,))],
+        compiler_params=pltpu.CompilerParams(vmem_limit_bytes=2 << 20),
+        cost_estimate=pl.CostEstimate(flops=0, bytes_accessed=5_000_000, transcendentals=0),
+    )(
+        pltpu.with_memory_space_constraint(res_raw, pltpu.VMEM),
+        pltpu.with_memory_space_constraint(new_raw, pltpu.VMEM),
+    )
+
     def whole(a):
         return a.reshape(NB, 4, 2, 128).transpose(2, 0, 1, 3).reshape(2, NB, NE)
 

time: 49.8 us -> 46.2 us (0.928)
  local copies, waits for them, and re-layouts: 2.95 us -> 0 us
  Pallas kernels: 46.1 us -> 45.4 us
    pallas_call x1, Pallas kernels: 46.1 us -> 43.1 us  [body(): pl.pallas_call(gather_kernel, out_shape=[pltpu.VMEM((NB * 8, 128), F32)]...]
    unnamed x2 -> x0, local copies, waits for them, and re-layouts: 2.95 us -> none
    pallas_call x0 -> x1, Pallas kernels: none -> 2.33 us  [body(): pl.pallas_call(write_kernel, out_shape=[jax.ShapeDtypeStruct((NB * 8, 128...]
where the time goes in v2:
time: 46.2 us; the launch traced here: 46 us
  Pallas kernels  45.4 us (98%)
  between operations  0.64 us (1%)
    pallas_call x1, Pallas kernels, body(): pl.pallas_call(gather_kernel, out_shape=[pltpu.VMEM((NB * 8, 128), F32)]...  43.1 us
    pallas_call x1, Pallas kernels, body(): pl.pallas_call(write_kernel, out_shape=[jax.ShapeDtypeStruct((NB * 8, 128...  2.33 us

profile of v2, /device:TPU:1, one launch (start us, length us, event | category | flops | bytes accessed | tf_op | source)
XLA Modules:
  0.0 46.0 jit_solution(1594544833688780638)
XLA Ops:
  0.6 43.1 %shard_map.122 = (f32[5000,128]{1,0:T(8,128)S(1)}, f32[5000,128]{1,0:T(8,128)S(1)}) custom-call(bf16[625,8,128]{2,1,0:T(8,128)(2,1)} %bitcast.22, bf16[625,8,512]{2,1,0:T(8,128)(2,1)} %bitcast.19, bf16[625,625]{1,0:T(8,128)(2,1)} %stiff_hbm.1, bf16[6,625,625]{2,1,0:T(8,128)(2,1)} %face_hbm.1, bf16[625,625]{1,0:T(8,128)(2,1)} %precond_hbm.1, ...), custom_call_target="tpu_custom_call" | custom-call | flops 12999999488 | bytes 16000000 | tf_op jit(solution)/shard_map/pallas_call | solution.py:490
  43.7 2.3 %shard_map.123 = (f32[5000,128]{1,0:T(8,128)}, f32[5000,128]{1,0:T(8,128)}) custom-call(f32[5000,128]{1,0:T(8,128)S(1)} %get-tuple-element.6.res_in, f32[5000,128]{1,0:T(8,128)S(1)} %get-tuple-element.7.new_in), custom_call_target="tpu_custom_call" | custom-call | bytes 5000000 | tf_op jit(solution)/shard_map/pallas_call | solution.py:556

commit v3 on v2

--- a/solution.py
+++ b/solution.py
@@ -49,25 +49,22 @@
     precond_hbm,
     deriv_hbm,
     volume_hbm,
-    step_hbm,
     amp_hbm,
     owner_hbm,
     links_hbm,
     res_ref,
-    new_ref,
+    change,
+    rounded,
+    pc_cols,
+    x,
     volume_ref,
-    step_ref,
     amp_ref,
     owner_ref,
     links_ref,
     acc,
-    rounded,
     pcv,
-    pc_cols,
-    change,
     xraw,
     xflat,
-    x,
     halo,
     halo_out,
     st_in,
@@ -126,7 +123,6 @@
                 (owner_hbm, owner_ref),
                 (links_hbm, links_ref),
                 (volume_hbm, volume_ref),
-                (step_hbm, step_ref),
             )
         )
     ]
@@ -441,15 +437,8 @@
                     res_ref[pl.ds(row * 8 + c * 2 + i, count, stride=8), :] = total[
                         0:count, c * 128 : (c + 1) * 128
                     ]
-            part = dot(pc_cols[:, base : base + 8 * size], rounded[i, base : base + 8 * size])
             if h == 0:
-                change[i] = part
-                continue
-            part = part + change[i]
-            for c in range(4):
-                lanes = slice(c * 128, (c + 1) * 128)
-                new = x[i, 0:NB, lanes].astype(F32) - step_ref[c : c + 1, :] * part[:, lanes]
-                new_ref[pl.ds(c * 2 + i, NB, stride=8), :] = new
+                change[i] = dot(pc_cols[:, 0:384], rounded[i, 0:384])
 
     for d in order:
         amp_copy(d).wait_send()
@@ -470,13 +459,26 @@
         halo_copy(1).wait_send()
 
 
-def write_kernel(res_in, new_in, res_hbm, new_hbm, sem):
+CHUNKS = ((0, 320), (320, 305))
+
+
+def finish_kernel(res_in, change, rounded, pc_cols, x, step_ref, res_hbm, new_hbm, new, sem):
     copies = [
-        pltpu.make_async_copy(res_in, res_hbm, sem.at[0]),
-        pltpu.make_async_copy(new_in, new_hbm, sem.at[1]),
+        pltpu.make_async_copy(res_in.at[pl.ds(8 * b, 8 * n)], res_hbm.at[pl.ds(8 * b, 8 * n)], sem.at[0, k])
+        for k, (b, n) in enumerate(CHUNKS)
     ]
     for copy in copies:
         copy.start()
+    for k, (b, n) in enumerate(CHUNKS):
+        for i in range(2):
+            part = dot(pc_cols[b : b + n, 384:640], rounded[i, 384:640]) + change[i, b : b + n]
+            for c in range(4):
+                lanes = slice(c * 128, (c + 1) * 128)
+                value = x[i, b : b + n, lanes].astype(F32) - step_ref[c : c + 1, :] * part[:, lanes]
+                new[pl.ds(8 * b + c * 2 + i, n, stride=8), :] = value
+        copy = pltpu.make_async_copy(new.at[pl.ds(8 * b, 8 * n)], new_hbm.at[pl.ds(8 * b, 8 * n)], sem.at[1, k])
+        copy.start()
+        copies.append(copy)
     for copy in copies:
         copy.wait()
 
@@ -487,25 +489,26 @@
     any_spec = pl.BlockSpec(memory_space=pl.ANY)
     vmem = pl.BlockSpec(memory_space=pltpu.VMEM)
     dma = pltpu.SemaphoreType.DMA
-    res_raw, new_raw = pl.pallas_call(
+    held = pl.pallas_call(
         gather_kernel,
-        out_shape=[pltpu.VMEM((NB * 8, 128), F32)] * 2,
-        in_specs=[any_spec] * 11,
-        out_specs=[vmem] * 2,
+        out_shape=[
+            pltpu.VMEM((NB * 8, 128), F32),
+            pltpu.VMEM((2, NB, NE), F32),
+            pltpu.VMEM((2, NBP, NE), BF16),
+            pltpu.VMEM((NB, NBP), BF16),
+            pltpu.VMEM((2, NBP, NE), BF16),
+        ],
+        in_specs=[any_spec] * 10,
+        out_specs=[vmem] * 5,
         scratch_shapes=[
-            pltpu.VMEM((4, 128), F32),
             pltpu.VMEM((4, 128), F32),
             pltpu.VMEM((2, 8), F32),
             pltpu.VMEM((64, 128), jnp.int32),
             pltpu.VMEM((6, NE), jnp.int32),
             pltpu.VMEM((2, NBP, NE), F32),
-            pltpu.VMEM((2, NBP, NE), BF16),
             pltpu.VMEM((NB, NB), BF16),
-            pltpu.VMEM((NB, NBP), BF16),
-            pltpu.VMEM((2, NB, NE), F32),
             pltpu.VMEM((NBP, 8, 128), BF16),
             pltpu.VMEM((GRP * 8, 128), F32),
-            pltpu.VMEM((2, NBP, NE), BF16),
             pltpu.VMEM((NBP, 256), BF16),
             pltpu.VMEM((2, NBP, 128), BF16),
             pltpu.VMEM((8, 2, GRP, NE), BF16),
@@ -537,7 +540,7 @@
             dma((2,)),
         ],
         compiler_params=pltpu.CompilerParams(
-            collective_id=0, has_side_effects=True, vmem_limit_bytes=56 << 20
+            collective_id=0, has_side_effects=True, vmem_limit_bytes=54 << 20
         ),
         cost_estimate=pl.CostEstimate(flops=13_000_000_000, bytes_accessed=16_000_000, transcendentals=0),
     )(
@@ -548,23 +551,19 @@
         precond,
         jnp.asarray(derivative_blocks()),
         volume.reshape(4, 128),
-        step_size.reshape(4, 128),
         amplitudes,
         surface_owner.reshape(64, 128),
         face_links,
     )
     res_raw, new_raw = pl.pallas_call(
-        write_kernel,
+        finish_kernel,
         out_shape=[jax.ShapeDtypeStruct((NB * 8, 128), F32)] * 2,
-        in_specs=[vmem] * 2,
+        in_specs=[vmem] * 6,
         out_specs=[any_spec] * 2,
-        scratch_shapes=[dma((2,))],
-        compiler_params=pltpu.CompilerParams(vmem_limit_bytes=2 << 20),
-        cost_estimate=pl.CostEstimate(flops=0, bytes_accessed=5_000_000, transcendentals=0),
-    )(
-        pltpu.with_memory_space_constraint(res_raw, pltpu.VMEM),
-        pltpu.with_memory_space_constraint(new_raw, pltpu.VMEM),
-    )
+        scratch_shapes=[pltpu.VMEM((NB * 8, 128), F32), dma((2, 2))],
+        compiler_params=pltpu.CompilerParams(vmem_limit_bytes=10 << 20),
+        cost_estimate=pl.CostEstimate(flops=330_000_000, bytes_accessed=5_000_000, transcendentals=0),
+    )(*[pltpu.with_memory_space_constraint(a, pltpu.VMEM) for a in held], step_size.reshape(4, 128))
 
     def whole(a):
         return a.reshape(NB, 4, 2, 128).transpose(2, 0, 1, 3).reshape(2, NB, NE)

time: 46.2 us -> 45.7 us (0.989)
  Pallas kernels: 45.4 us -> 44.9 us
    pallas_call x2, Pallas kernels: 45.4 us -> 44.9 us  [the longest x1 42.5 us: body(): pl.pallas_call(gather_kernel, out_shape=[pltpu.VMEM((NB * 8, 128), F32),...]
where the time goes in v3:
time: 45.7 us; the launch traced here: 45.6 us
  Pallas kernels  44.9 us (98%)
  between operations  0.66 us (1%)
    pallas_call x1, Pallas kernels, body(): pl.pallas_call(gather_kernel, out_shape=[pltpu.VMEM((NB * 8, 128), F32),...  42.5 us
    pallas_call x1, Pallas kernels, body(): pl.pallas_call(finish_kernel, out_shape=[jax.ShapeDtypeStruct((NB * 8, 12...  2.36 us

profile of v3, /device:TPU:1, one launch (start us, length us, event | category | flops | bytes accessed | tf_op | source)
XLA Modules:
  0.0 45.6 jit_solution(4467162904652414124)
XLA Ops:
  0.6 0.0 copy-start
  0.6 42.5 %shard_map.122 = (f32[5000,128]{1,0:T(8,128)S(1)}, f32[2,625,512]{2,1,0:T(8,128)S(1)}, bf16[2,640,512]{2,1,0:T(8,128)(2,1)S(1)}, bf16[625,640]{1,0:T(8,128)(2,1)S(1)}, bf16[2,640,512]{2,1,0:T(8,128)(2,1)S(1)}) custom-call(bf16[625,8,128]{2,1,0:T(8,128)(2,1)} %bitcast.23, bf16[625,8,512]{2,1,0:T(8,128)(2,1)} %bitcast.20, bf16[625,625]{1,0:T(8,128)(2,1)} %stiff_hbm.1, ...), custom_call_target="tpu_custom_call" | custom-call | flops 12999999488 | bytes 16000000 | tf_op jit(solution)/shard_map/pallas_call | solution.py:492
  43.2 0.0 copy-done
  43.2 2.4 %shard_map.123 = (f32[5000,128]{1,0:T(8,128)}, f32[5000,128]{1,0:T(8,128)}) custom-call(f32[5000,128]{1,0:T(8,128)S(1)} %get-tuple-element.9.res_in, f32[2,625,512]{2,1,0:T(8,128)S(1)} %get-tuple-element.10.change, bf16[2,640,512]{2,1,0:T(8,128)(2,1)S(1)} %get-tuple-element.11.rounded, bf16[625,640]{1,0:T(8,128)(2,1)S(1)} %get-tuple-element.12.pc_cols, ...), custom_call_target="tpu_custom_call" | custom-call | flops 330000000 | bytes 5000000 | tf_op jit(solution)/shard_map/pallas_call | solution.py:558
Async XLA Ops:
  0.6 42.6 %copy-start = (f32[512]{0:T(512)S(1)}, f32[512]{0:T(512)}, u32[]{:S(2)}) copy-start(f32[512]{0:T(512)} %param.13) | copy-start | bytes 6148

commit v4 on v3

--- a/solution.py
+++ b/solution.py
@@ -291,13 +291,6 @@
             device_id_type=MESH,
         )
 
-    @pl.when(slab < 15)
-    def _():
-        halo_copy(0).start()
-
-    @pl.when(slab > 0)
-    def _():
-        halo_copy(1).start()
 
     for d in range(8):
         ms_copy(d, True).start()
@@ -306,6 +299,14 @@
     for h in range(FIRST_PIECES, len(PIECES)):
         for d in order:
             state_copy(h, d).start()
+
+    @pl.when(slab < 15)
+    def _():
+        halo_copy(0).start()
+
+    @pl.when(slab > 0)
+    def _():
+        halo_copy(1).start()
     ms_self = local(
         snd_own.at[pl.ds(pl.multiple_of(mine * 32, 32), 32), :],
         ms_in.at[pl.ds(pl.multiple_of(slab * 32, 32), 32), :],

time: 45.7 us -> 45.4 us (level)
  no operation moved by 1% of the time
where the time goes in v4:
time: 45.4 us; the launch traced here: 45.2 us
  Pallas kernels  44.6 us (98%)
  between operations  0.66 us (1%)
    pallas_call x1, Pallas kernels, body(): pl.pallas_call(gather_kernel, out_shape=[pltpu.VMEM((NB * 8, 128), F32),...  42.2 us
    pallas_call x1, Pallas kernels, body(): pl.pallas_call(finish_kernel, out_shape=[jax.ShapeDtypeStruct((NB * 8, 12...  2.36 us

profile of v4, /device:TPU:1, one launch (start us, length us, event | category | flops | bytes accessed | tf_op | source)
XLA Modules:
  0.0 45.2 jit_solution(16109578905866121322)
XLA Ops:
  0.6 0.0 copy-start
  0.6 42.2 %shard_map.122 = (f32[5000,128]{1,0:T(8,128)S(1)}, f32[2,625,512]{2,1,0:T(8,128)S(1)}, bf16[2,640,512]{2,1,0:T(8,128)(2,1)S(1)}, bf16[625,640]{1,0:T(8,128)(2,1)S(1)}, bf16[2,640,512]{2,1,0:T(8,128)(2,1)S(1)}) custom-call(bf16[625,8,128]{2,1,0:T(8,128)(2,1)} %bitcast.23, bf16[625,8,512]{2,1,0:T(8,128)(2,1)} %bitcast.20, bf16[625,625]{1,0:T(8,128)(2,1)} %stiff_hbm.1, ...), custom_call_target="tpu_custom_call" | custom-call | flops 12999999488 | bytes 16000000 | tf_op jit(solution)/shard_map/pallas_call | solution.py:493
  42.8 0.0 copy-done
  42.9 2.4 %shard_map.123 = (f32[5000,128]{1,0:T(8,128)}, f32[5000,128]{1,0:T(8,128)}) custom-call(f32[5000,128]{1,0:T(8,128)S(1)} %get-tuple-element.9.res_in, f32[2,625,512]{2,1,0:T(8,128)S(1)} %get-tuple-element.10.change, bf16[2,640,512]{2,1,0:T(8,128)(2,1)S(1)} %get-tuple-element.11.rounded, bf16[625,640]{1,0:T(8,128)(2,1)S(1)} %get-tuple-element.12.pc_cols, ...), custom_call_target="tpu_custom_call" | custom-call | flops 330000000 | bytes 5000000 | tf_op jit(solution)/shard_map/pallas_call | solution.py:559
Async XLA Ops:
  0.6 42.2 %copy-start = (f32[512]{0:T(512)S(1)}, f32[512]{0:T(512)}, u32[]{:S(2)}) copy-start(f32[512]{0:T(512)} %param.13) | copy-start | bytes 6148

commit v5 on v4

--- a/solution.py
+++ b/solution.py
@@ -130,7 +130,7 @@
     def peer(d):
         return ((zz + d // 2) % 4) * 2 + (yl + d % 2) % 2
 
-    order = (4, 5, 2, 6, 3, 7, 1)
+    order = (5, 3, 7, 4, 2, 6, 1)
     barrier = pltpu.get_barrier_semaphore()
 
     def greet(i, s):

time: 45.4 us -> 45.4 us (level)
  no operation moved by 1% of the time
where the time goes in v5:
time: 45.4 us; the launch traced here: 45.2 us
  Pallas kernels  44.6 us (98%)
  between operations  0.66 us (1%)
    pallas_call x1, Pallas kernels, body(): pl.pallas_call(gather_kernel, out_shape=[pltpu.VMEM((NB * 8, 128), F32),...  42.2 us
    pallas_call x1, Pallas kernels, body(): pl.pallas_call(finish_kernel, out_shape=[jax.ShapeDtypeStruct((NB * 8, 12...  2.36 us

profile of v5, /device:TPU:1, one launch (start us, length us, event | category | flops | bytes accessed | tf_op | source)
XLA Modules:
  0.0 45.2 jit_solution(7931597153514216757)
XLA Ops:
  0.6 0.0 copy-start
  0.6 42.2 %shard_map.122 = (f32[5000,128]{1,0:T(8,128)S(1)}, f32[2,625,512]{2,1,0:T(8,128)S(1)}, bf16[2,640,512]{2,1,0:T(8,128)(2,1)S(1)}, bf16[625,640]{1,0:T(8,128)(2,1)S(1)}, bf16[2,640,512]{2,1,0:T(8,128)(2,1)S(1)}) custom-call(bf16[625,8,128]{2,1,0:T(8,128)(2,1)} %bitcast.23, bf16[625,8,512]{2,1,0:T(8,128)(2,1)} %bitcast.20, bf16[625,625]{1,0:T(8,128)(2,1)} %stiff_hbm.1, ...), custom_call_target="tpu_custom_call" | custom-call | flops 12999999488 | bytes 16000000 | tf_op jit(solution)/shard_map/pallas_call | solution.py:493
  42.9 0.0 copy-done
  42.9 2.4 %shard_map.123 = (f32[5000,128]{1,0:T(8,128)}, f32[5000,128]{1,0:T(8,128)}) custom-call(f32[5000,128]{1,0:T(8,128)S(1)} %get-tuple-element.9.res_in, f32[2,625,512]{2,1,0:T(8,128)S(1)} %get-tuple-element.10.change, bf16[2,640,512]{2,1,0:T(8,128)(2,1)S(1)} %get-tuple-element.11.rounded, bf16[625,640]{1,0:T(8,128)(2,1)S(1)} %get-tuple-element.12.pc_cols, ...), custom_call_target="tpu_custom_call" | custom-call | flops 330000000 | bytes 5000000 | tf_op jit(solution)/shard_map/pallas_call | solution.py:559
Async XLA Ops:
  0.6 42.2 %copy-start = (f32[512]{0:T(512)S(1)}, f32[512]{0:T(512)}, u32[]{:S(2)}) copy-start(f32[512]{0:T(512)} %param.13) | copy-start | bytes 6148
